TPU v7x, 512 devices: a whole 4x4x16 slice. The times are simulated.
512 devices in a mesh: band: 32 (over y, x, core), work: 16 (over z).
Axes of the slice: x: 4, y: 4, z: 16, core: 2. Of those that a mesh axis runs over, the one named last changes fastest.
Arguments:
- mask_logits: float32 [1536, 4096], P('band', 'work'), may hold values from -6 to 6
- loss_weights: float32 [1536, 4096], P('band', 'work'), may hold values from 0.1 to 6, as said below
- target_bits: int32 [1536, 4096], P('band', 'work'), may hold values 0 or 1
- kernels: bfloat16 [24, 25, 25], replicated, may hold values from -0.25 to 0.25
- kernel_gains: float32 [12], replicated, may hold values from 0.02 to 0.2
- imager_list: int32 [32, 16, 2, 1], P('band'), may hold values from 0 to 16, as said below
Outputs:
- final_logits: float32 [1536, 4096], P('band', 'work')
Inputs may be any that keep to these rules, and one draw needn't show every extreme that they name: `imager_list`: an entry 16 marks a tile without pattern, which is not imaged; in every row group some device has both its tiles with pattern. `loss_weights`: positive weights.
All inputs are finite; a program needn't handle non-finite values. No bound on the sum of `target_bits` on one device may be relied on, other than what follows from the above.
Results may differ from a plain program's by a relative error of at most 0.0045.
Values may be sent and summed in bfloat16 or wider, within the bound.
A program may use at most 64 MiB of HBM per device.

v0:
```python
import jax
import jax.numpy as jnp
from jax import lax
from jax.sharding import PartitionSpec as P

TR = 24
TC = 256
ITERS = 2


STEEP = 4.0
THRESH = 0.5
STEP_SIZE = 0.5
EPSILON = 1e-06


def extended(block, sides, width):
    for axis, dim in sides:
        count = lax.axis_size(axis)
        forward = [(i, i + 1) for i in range(count - 1)]
        backward = [(target, source) for source, target in forward]
        low = lax.ppermute(
            lax.slice_in_dim(block, block.shape[dim] - width, None, axis=dim), axis, forward
        )
        high = lax.ppermute(lax.slice_in_dim(block, 0, width, axis=dim), axis, backward)
        block = jnp.concatenate([low, block, high], axis=dim)
    return block


def image_tile(flat, kernels, sigma_both, halo_width):
    kernel_taps = 2 * halo_width + 1
    tile_rows = TR
    tile_cols = TC
    padded_rows = tile_rows + 2 * halo_width
    padded_cols = tile_cols + 2 * halo_width
    padded_size = padded_rows * padded_cols
    inner_size = tile_rows * tile_cols
    padded = flat[:padded_size].reshape(padded_rows, padded_cols)
    weight_v = (
        flat[padded_size : padded_size + inner_size]
        .reshape(tile_rows, tile_cols)
        .astype(jnp.float32)
    )
    weight_t = flat[padded_size + inner_size :].reshape(tile_rows, tile_cols).astype(jnp.float32)
    shifted = jnp.stack(
        [padded[:, offset_col : offset_col + tile_cols] for offset_col in range(kernel_taps)],
        axis=0,
    )
    fields = jnp.zeros((kernels.shape[0], tile_rows, tile_cols), jnp.float32)
    for offset_row in range(kernel_taps):
        fields = fields + jnp.einsum(
            "cd,dyx->cyx",
            kernels[:, offset_row, :],
            shifted[:, offset_row : offset_row + tile_rows, :],
            preferred_element_type=jnp.float32,
        )
    intensity = jnp.sum(sigma_both[:, None, None] * fields * fields, axis=0)
    resist = jax.nn.sigmoid(STEEP * (intensity - THRESH))
    slopes = 2.0 * (weight_v * resist - weight_t) * STEEP * resist * (1.0 - resist)
    field_grad = (2.0 * sigma_both[:, None, None] * fields * slopes[None]).astype(jnp.bfloat16)
    spread_sum = jnp.zeros((kernel_taps, padded_rows, tile_cols), jnp.float32)
    for offset_row in range(kernel_taps):
        spread = jnp.einsum(
            "cd,cyx->dyx", kernels[:, offset_row, :], field_grad, preferred_element_type=jnp.float32
        )
        spread_sum = spread_sum.at[:, offset_row : offset_row + tile_rows, :].add(spread)
    mask_grad = jnp.zeros((padded_rows, padded_cols), jnp.float32)
    for offset_col in range(kernel_taps):
        mask_grad = mask_grad.at[:, offset_col : offset_col + tile_cols].add(spread_sum[offset_col])
    return mask_grad.reshape(padded_size)


def image_slots(stacked, filled, kernels, sigma_both, halo_width):
    slot_count = stacked.shape[0]
    padded_size = (TR + 2 * halo_width) * (TC + 2 * halo_width)
    filled_int = filled.astype(jnp.int32)
    position = jnp.cumsum(filled_int) - filled_int
    column_ids = lax.broadcasted_iota(jnp.int32, (slot_count, slot_count), 1)
    selector = jnp.logical_and(filled[:, None], position[:, None] == column_ids)
    packed = jnp.einsum(
        "jp,jf->pf", selector.astype(jnp.bfloat16), stacked, preferred_element_type=jnp.bfloat16
    )
    filled_count = jnp.sum(filled_int)

    def image_step(turn_index, tile_grads):
        flat = lax.dynamic_slice_in_dim(packed, turn_index, 1, 0)[0]
        result = image_tile(flat, kernels, sigma_both, halo_width)
        return lax.dynamic_update_slice_in_dim(tile_grads, result[None], turn_index, 0)

    tile_grads = lax.fori_loop(
        0, filled_count, image_step, jnp.zeros((slot_count, padded_size), jnp.float32)
    )
    return jnp.dot(
        selector.astype(jnp.float32),
        tile_grads,
        precision=lax.Precision.HIGHEST,
        preferred_element_type=jnp.float32,
    )


def shards(mask_logits, loss_weights, target_bits, kernels, kernel_gains, imager_list):
    kernel_taps = kernels.shape[1]
    halo_width = (kernel_taps - 1) // 2
    height, tile_cols = mask_logits.shape
    tile_count = height // TR
    padded_rows = TR + 2 * halo_width
    padded_cols = tile_cols + 2 * halo_width
    padded_size = padded_rows * padded_cols
    inner_size = TR * tile_cols
    imagers = lax.axis_size("work")
    own_index = lax.axis_index("work")
    cells_total = height * tile_cols * lax.axis_size("band") * imagers
    sigma_both = jnp.concatenate([kernel_gains, kernel_gains])
    listed = imager_list[0, :, :, 0]
    live_tiles = listed < imagers
    device_ids = lax.broadcasted_iota(jnp.int32, (imagers, tile_count), 0)
    mine = device_ids == own_index
    own_live = jnp.sum(jnp.where(mine, live_tiles.astype(jnp.int32), 0), axis=0) > 0
    weight_v = loss_weights.astype(jnp.bfloat16)
    weight_t = (weight_v.astype(jnp.float32) * target_bits.astype(jnp.float32)).astype(jnp.bfloat16)
    weight_pack = jnp.concatenate(
        [weight_v.reshape(tile_count, inner_size), weight_t.reshape(tile_count, inner_size)], axis=1
    )
    logits = mask_logits
    for iteration in range(ITERS):
        soft = jax.nn.sigmoid(logits)
        mask_cells = soft.astype(jnp.bfloat16)
        framed = extended(mask_cells, (("band", 0), ("work", 1)), halo_width)
        padded = jnp.stack(
            [framed[tile * TR : tile * TR + padded_rows] for tile in range(tile_count)], axis=0
        ).reshape(tile_count, padded_size)
        payload = jnp.concatenate([padded, weight_pack], axis=1)
        tile_grads = image_slots(payload, own_live, kernels, sigma_both, halo_width).reshape(
            tile_count, padded_rows, padded_cols
        )
        framed_grad = jnp.zeros((height + 2 * halo_width, padded_cols), jnp.float32)
        for tile in range(tile_count):
            framed_grad = framed_grad.at[tile * TR : tile * TR + padded_rows].add(tile_grads[tile])
        middle_gap = jnp.zeros((height + 2 * halo_width, tile_cols - 2 * halo_width), jnp.float32)
        side_rims = jnp.concatenate(
            [framed_grad[:, :halo_width], middle_gap, framed_grad[:, padded_cols - halo_width :]],
            axis=1,
        )
        side_extended = extended(side_rims.astype(jnp.bfloat16), (("work", 1),), halo_width).astype(
            side_rims.dtype
        )
        columns = framed_grad[:, halo_width : halo_width + tile_cols] + jnp.concatenate(
            [
                side_extended[:, :halo_width],
                middle_gap,
                side_extended[:, padded_cols - halo_width :],
            ],
            axis=1,
        )
        row_gap = jnp.zeros((height - 2 * halo_width, tile_cols), jnp.float32)
        edge_rims = jnp.concatenate(
            [columns[:halo_width], row_gap, columns[height + halo_width :]], axis=0
        )
        edge_extended = extended(edge_rims.astype(jnp.bfloat16), (("band", 0),), halo_width).astype(
            edge_rims.dtype
        )
        inner_grad = columns[halo_width : halo_width + height] + jnp.concatenate(
            [edge_extended[:halo_width], row_gap, edge_extended[height + halo_width :]], axis=0
        )
        gradient = inner_grad * soft * (1.0 - soft)
        squares_total = lax.psum(jnp.sum(gradient * gradient), ("band", "work"))
        logits = logits - STEP_SIZE / jnp.sqrt(squares_total / cells_total + EPSILON) * gradient
    return logits


def solution(mesh):
    in_specs = (
        P("band", "work"),
        P("band", "work"),
        P("band", "work"),
        P(),
        P(),
        P("band", None, None, None),
    )
    out_specs = P("band", "work")
    return jax.shard_map(shards, mesh=mesh, in_specs=in_specs, out_specs=out_specs, check_vma=False)
```

profile of v0, /device:TPU:1, one launch (start us, length us, event | category | flops | bytes accessed | tf_op | source)
XLA Modules:
  0.0 532.6 jit_solution(2826709997388840967)
XLA Ops:
  0.9 4.5 collective-permute-start
  5.4 5.6 %collective-permute-start.1 = (bf16[12,256]{1,0:T(8,128)(2,1)S(1)}, bf16[12,256]{1,0:T(8,128)(2,1)S(1)}, u32[]{:S(2)}, u32[]{:S(2)}) collective-permute-start(bf16[12,256]{1,0:T(8,128)(2,1)S(1)} %get-tuple-element.2842), channel_id=1, source_target_pairs={{16,0},{32,16},{48,32},{64,48},{80,64},{96,80},{112,96},{128,112},... | collective-permute-start | bytes 18440 | tf_op jit(solution)/shard_map/ppermute | solution.py:25
  26.9 115.8 %while.132 = (s32[]{:T(128)}, f32[2,13440]{1,0:T(2,128)S(1)}, s32[]{:T(128)}, f32[24]{0:T(128)S(1)}, bf16[2,25728]{1,0:T(2,128)(2,1)S(1)}, /*index=5*/bf16[24,25...) while((s32[]{:T(128)}, f32[2,13440]{1,0:T(2,128)S(1)}, ...), condition=%wide.region_30.31_spmd, body=%wide.region_27.0_spmd.sunk | while | flops 377425952 | bytes 110220120 | solution.py:90
  29.4 2.0 stack.442
  86.8 2.0 stack.442
  145.0 1.3 collective-permute-start.5
  146.4 3.1 collective-permute-done.5
  149.8 1.9 collective-permute-start.6
  151.8 5.1 collective-permute-start.7
  157.0 1.3 collective-permute-done.7
  159.3 114.3 %psum.14 = f32[]{:T(128)} all-reduce(f32[]{:T(128)} %get-tuple-element.2705), channel_id=1, replica_groups=mesh['band'=32,'work'=16] {'band','work'}, use_global_device_ids=true, to_apply=%region_32.33 | all-reduce | flops 1 | bytes 8 | tf_op jit(solution)/shard_map/psum | solution.py:166
  274.4 2.7 collective-permute-start.8
  277.1 1.9 collective-permute-start.9
  279.0 3.0 collective-permute-done.9
  282.1 2.7 collective-permute-start.10
  286.2 3.2 collective-permute-done.11
  290.2 116.0 %while.133 = (s32[]{:T(128)}, f32[2,13440]{1,0:T(2,128)S(1)}, s32[]{:T(128)}, f32[24]{0:T(128)S(1)}, bf16[2,25728]{1,0:T(2,128)(2,1)S(1)}, /*index=5*/bf16[24,25...) while((s32[]{:T(128)}, f32[2,13440]{1,0:T(2,128)S(1)}, ...), condition=%wide.region_36.37_spmd, body=%wide.region_33.0_spmd.sunk | while | flops 377425952 | bytes 110220120 | solution.py:90
  292.9 2.0 stack.443
  350.3 2.0 stack.443
  409.7 3.2 collective-permute-done.13
  413.3 1.9 collective-permute-start.14
  415.2 3.3 collective-permute-start.15
  418.5 1.6 collective-permute-done.15
  421.1 109.9 %psum.15 = f32[]{:T(128)} all-reduce(f32[]{:T(128)} %get-tuple-element.2701), channel_id=1, replica_groups=mesh['band'=32,'work'=16] {'band','work'}, use_global_device_ids=true, to_apply=%region_38.39 | all-reduce | flops 1 | bytes 8 | tf_op jit(solution)/shard_map/psum | solution.py:166
  (664 shorter events, 242.5 us)
Async XLA Ops:
  0.0 26.9 %copy-start = (bf16[24,25,25]{2,0,1:T(8,128)(2,1)S(1)}, bf16[24,25,25]{2,0,1:T(8,128)(2,1)}, u32[]{:S(2)}) copy-start(bf16[24,25,25]{2,0,1:T(8,128)(2,1)} %param.221) | copy-start | bytes 90004
  0.9 18.3 %collective-permute-start = (bf16[12,256]{1,0:T(8,128)(2,1)S(1)}, bf16[12,256]{1,0:T(8,128)(2,1)S(1)}, u32[]{:S(2)}, u32[]{:S(2)}) collective-permute-start(bf16[12,256]{1,0:T(8,128)(2,1)S(1)} %get-tuple-element.2841), channel_id=1, source_target_pairs={{0,16},{16,32},{32,48},{48,64},{64,80},{80,96},{96,112},{112,128},... | collective-permute-start | bytes 18440 | tf_op jit(solution)/shard_map/ppermute | solution.py:22
  5.4 13.8 %collective-permute-start.1 = (bf16[12,256]{1,0:T(8,128)(2,1)S(1)}, bf16[12,256]{1,0:T(8,128)(2,1)S(1)}, u32[]{:S(2)}, u32[]{:S(2)}) collective-permute-start(bf16[12,256]{1,0:T(8,128)(2,1)S(1)} %get-tuple-element.2842), channel_id=1, source_target_pairs={{16,0},{32,16},{48,32},{64,48},{80,64},{96,80},{112,96},{128,112},... | collective-permute-start | bytes 18440 | tf_op jit(solution)/shard_map/ppermute | solution.py:25
  19.3 6.8 %collective-permute-start.2 = (bf16[72,12]{1,0:T(8,128)(2,1)S(1)}, bf16[72,12]{1,0:T(8,128)(2,1)S(1)}, u32[]{:S(2)}, u32[]{:S(2)}) collective-permute-start(bf16[72,12]{1,0:T(8,128)(2,1)S(1)} %get-tuple-element.2837), channel_id=1, source_target_pairs={{0,1},{1,2},{2,3},{3,4},{4,5},{5,6},{6,7},{7,8},{8,9},{9,10},{10,1... | collective-permute-start | bytes 5192 | tf_op jit(solution)/shard_map/ppermute | solution.py:22
  20.5 5.5 %collective-permute-start.3 = (bf16[72,12]{1,0:T(8,128)(2,1)S(1)}, bf16[72,12]{1,0:T(8,128)(2,1)S(1)}, u32[]{:S(2)}, u32[]{:S(2)}) collective-permute-start(bf16[72,12]{1,0:T(8,128)(2,1)S(1)} %get-tuple-element.2838), channel_id=1, source_target_pairs={{1,0},{2,1},{3,2},{4,3},{5,4},{6,5},{7,6},{8,7},{9,8},{10,9},{11,1... | collective-permute-start | bytes 5192 | tf_op jit(solution)/shard_map/ppermute | solution.py:25
  142.7 15.8 %copy-start.1 = (f32[48,256]{1,0:T(8,128)S(1)}, f32[48,256]{1,0:T(8,128)}, u32[]{:S(2)}) copy-start(f32[48,256]{1,0:T(8,128)} %param.218) | copy-start | bytes 147460
  143.7 2.7 collective-permute-start.4
  145.0 4.5 collective-permute-start.5
  149.8 7.1 %collective-permute-start.6 = (bf16[12,256]{1,0:T(8,128)(2,1)S(1)}, bf16[12,256]{1,0:T(8,128)(2,1)S(1)}, u32[]{:S(2)}, u32[]{:S(2)}) collective-permute-start(bf16[12,256]{1,0:T(8,128)(2,1)S(1)} %get-tuple-element.2836), channel_id=1, source_target_pairs={{0,16},{16,32},{32,48},{48,64},{64,80},{80,96},{96,112},{112,128},... | collective-permute-start | bytes 18440 | tf_op jit(solution)/shard_map/ppermute | solution.py:22
  151.8 6.5 %collective-permute-start.7 = (bf16[12,256]{1,0:T(8,128)(2,1)S(1)}, bf16[12,256]{1,0:T(8,128)(2,1)S(1)}, u32[]{:S(2)}, u32[]{:S(2)}) collective-permute-start(bf16[12,256]{1,0:T(8,128)(2,1)S(1)} %get-tuple-element.2835), channel_id=1, source_target_pairs={{16,0},{32,16},{48,32},{64,48},{80,64},{96,80},{112,96},{128,112},... | collective-permute-start | bytes 18440 | tf_op jit(solution)/shard_map/ppermute | solution.py:25
  274.4 4.6 collective-permute-start.8
  277.1 5.0 collective-permute-start.9
  282.1 4.0 collective-permute-start.10
  284.9 4.5 collective-permute-start.11
  407.1 2.6 collective-permute-start.12
  408.4 4.5 collective-permute-start.13
  413.3 5.3 collective-permute-start.14
  415.2 5.0 collective-permute-start.15
where the time goes:
time: 534 us; the launch traced here: 533 us
  blocking collectives  224 us (42%)
  local copies, waits for them, and re-layouts  92.4 us (17%)
  other arithmetic  89.4 us (17%)
  matrix products  61.2 us (11%)
  starting transfers between devices  38.6 us (7%)
  waiting for transfers between devices  15.5 us (3%)
  loops' own time  9.08 us (2%)
    psum x2, blocking collectives, shards(): squares_total = lax.psum(jnp.sum(gradient * gradient), ('band', 'work'))  224 us
    another operation x121, other arithmetic  80.9 us
    scatter-add x100, local copies, waits for them, and re-layouts, image_tile(): mask_grad.at[:, offset_col:offset_col + tile_cols]  65.5 us
    dot_general x100, matrix products, image_tile(): jnp.einsum('cd,cyx->dyx', kernels[:, offset_row, :], field_grad, preferre...  36.9 us
    dot_general x100, matrix products, image_tile(): jnp.einsum('cd,dyx->cyx', kernels[:, offset_row, :], shifted[:, offset_ro...  23 us
    ppermute x8, starting transfers between devices, extended(): lax.ppermute(lax.slice_in_dim(block, 0, width, axis=dim), axis, backward)  21.1 us
    ppermute x8, starting transfers between devices, extended(): lax.ppermute(lax.slice_in_dim(block, block.shape[dim] - width, None, axis...  17.6 us
    ppermute x8, waiting for transfers between devices, extended(): lax.ppermute(lax.slice_in_dim(block, 0, width, axis=dim), axis, backward)  15.5 us
  transfers between devices with their start and end apart: 16, of which 6 were waited for; matrix products, arithmetic and copies ran while one was open for 2% of the time, Pallas kernels for 0%

commit v1 on v0

v1 whole, which is shorter than its diff:
```python
import functools

import jax
import jax.numpy as jnp
from jax import lax
from jax.experimental import pallas as pl
from jax.experimental.pallas import tpu as pltpu
from jax.sharding import PartitionSpec as P

MESH = pl.DeviceIdType.MESH
TR = 24
H, W = 48, 256
K2 = 24
KS = 25
JP = 26
HALO = 24
ER, EC = 72, 384
LR, LC = 96, 512
OWN_R, OWN_C = 24, 128
KF = 4 * JP * 8
KFP = 896
KB = 4 * K2 * 8
ITERS = 2
STEEP, THRESH, STEP_SIZE, EPSILON = 4.0, 0.5, 0.5, 1e-6


def sigmoid(x):
    return 1.0 / (1.0 + jnp.exp(-x))


def kernel(
    nb, nw, log_ref, lw_ref, bits_ref, kf_ref, kb_ref, gain_ref, img_ref, out_ref,
    frame, gframe, vown, vframe, vext, tmat, umat, sblk, gblk, slots_c, slots_b, slots_w, part,
    a_send, a_recv, v_send, v_recv, g_send, g_recv, r_send, r_recv,
):
    b, w = lax.axis_index("band"), lax.axis_index("work")
    up, down = lax.rem(b + nb - 1, nb), lax.rem(b + 1, nb)
    left, right = lax.rem(w + nw - 1, nw), lax.rem(w + 1, nw)

    core = lax.rem(b, 2)

    def other_core(k):
        return (b + 1 - 2 * core, w)

    def same_core(k):
        return (lax.rem(b + 2 * k, nb), w)

    def along_work(k):
        return (b, lax.rem(w + k, nw))

    barrier = pltpu.get_barrier_semaphore()
    greeted = [along_work(k) for k in range(1, nw)] + [same_core(k) for k in range(1, nb // 2)]
    greeted += [(up, w), (down, w), (up, left), (up, right), (down, left), (down, right)]
    for dev in greeted:
        pl.semaphore_signal(barrier, inc=1, device_id=dev, device_id_type=MESH)

    rows = lax.broadcasted_iota(jnp.int32, (H, W), 0)
    live0 = jnp.where(img_ref[w * 2] < nw, 1.0, 0.0)
    live1 = jnp.where(img_ref[w * 2 + 1] < nw, 1.0, 0.0)
    weight = lw_ref[...].astype(jnp.bfloat16).astype(jnp.float32)
    weight = weight * jnp.where(rows < TR, live0, live1)
    vown[...] = jnp.where(bits_ref[...] == 1, -weight, weight).astype(jnp.bfloat16)

    pl.semaphore_wait(barrier, len(greeted))

    def frames(src, dst, h, top, send, recv):
        lo, hi = slice(0, h), slice(H - h, H)
        first, last = slice(0, 128), slice(W - 128, W)
        above, below = slice(top - h, top), slice(top + H, top + H + h)
        mid = slice(top, top + H)
        before, after, centre = slice(0, 128), slice(128 + W, 256 + W), slice(128, 128 + W)
        plan = (
            (lo, slice(0, W), below, centre, (up, w)),
            (hi, slice(0, W), above, centre, (down, w)),
            (slice(0, H), first, mid, after, (b, left)),
            (slice(0, H), last, mid, before, (b, right)),
            (lo, first, below, after, (up, left)),
            (lo, last, below, before, (up, right)),
            (hi, first, above, after, (down, left)),
            (hi, last, above, before, (down, right)),
        )
        copies = []
        for k, (sr, sc, dr, dc, dev) in enumerate(plan):
            copies.append(
                pltpu.make_async_remote_copy(
                    src.at[sr, sc], dst.at[dr, dc], send.at[k], recv.at[k], dev, MESH
                )
            )
        for copy in copies:
            copy.start()
        return copies

    copies_v = frames(vown, vframe, 16, 16, v_send, v_recv)
    copies_a = frames(log_ref, frame, HALO, OWN_R, a_send, a_recv)
    frame[OWN_R : OWN_R + H, OWN_C : OWN_C + W] = log_ref[...]
    vframe[16 : 16 + H, 128 : 128 + W] = vown[...]

    lane_f = lax.broadcasted_iota(jnp.int32, (8, KFP), 1) & 7
    sub_f = lax.broadcasted_iota(jnp.int32, (8, KFP), 0)
    lane_b = lax.broadcasted_iota(jnp.int32, (8, KB), 1) & 7
    sub_b = lax.broadcasted_iota(jnp.int32, (8, KB), 0)

    def toeplitz(row, lane, sub, step):
        wide = jnp.broadcast_to(row.astype(jnp.float32), lane.shape)
        same = pltpu.roll(wide, 0, 1, stride=1, stride_axis=0)
        prior = pltpu.roll(wide, step - 8, 1, stride=1, stride_axis=0)
        return jnp.where(lane >= sub, same, prior)

    for c in range(0, K2, 2):
        pair = [toeplitz(kf_ref[c + d : c + d + 1, :], lane_f, sub_f, JP * 8) for d in range(2)]
        tmat[8 * c : 8 * c + 16, :] = jnp.concatenate(pair, axis=0)[:, :KF].astype(jnp.bfloat16)
    for j in range(0, JP, 2):
        pair = [toeplitz(kb_ref[j + d : j + d + 1, :], lane_b, sub_b, K2 * 8) for d in range(2)]
        umat[8 * j : 8 * j + 16, :] = jnp.concatenate(pair, axis=0).astype(jnp.bfloat16)

    for copy in copies_v:
        copy.wait_recv()
    band_row = b * H + lax.broadcasted_iota(jnp.int32, (ER, EC), 0) - 12
    band_col = w * W + lax.broadcasted_iota(jnp.int32, (ER, EC), 1) - 12
    inside = (band_row >= 0) & (band_row < nb * H) & (band_col >= 0) & (band_col < nw * W)
    signed = vframe[...].astype(jnp.float32)
    signed = pltpu.roll(signed, LC - 116, 1)[4 : 4 + ER, :EC]
    vext[...] = jnp.where(inside, signed, 0.0)

    for copy in copies_a:
        copy.wait_recv()

    band_row = b * H + lax.broadcasted_iota(jnp.int32, (LR, LC), 0) - OWN_R
    band_col = w * W + lax.broadcasted_iota(jnp.int32, (LR, LC), 1) - OWN_C
    inside = (band_row >= 0) & (band_row < nb * H) & (band_col >= 0) & (band_col < nw * W)

    sends = list(copies_v) + list(copies_a)
    for step in range(ITERS):
        soft = sigmoid(frame[...])
        own_soft = soft[OWN_R : OWN_R + H, OWN_C : OWN_C + W]
        mask = jnp.where(inside, soft.astype(jnp.bfloat16).astype(jnp.float32), 0.0)
        for j in range(0, JP, 2):
            pair = [
                pltpu.roll(mask, LC - 104 - min(j + d, KS - 1), 1)[:, :EC].reshape(LR // 8, 8, EC)
                for d in range(2)
            ]
            sblk[:, 8 * j : 8 * j + 16, :] = jnp.concatenate(pair, axis=1).astype(jnp.bfloat16)

        def forward(blk, carry):
            window = sblk[pl.ds(blk, 4)].reshape(KF, EC)
            fields = jnp.dot(tmat[...], window, preferred_element_type=jnp.float32)
            fields = fields.reshape(K2, 8, EC)
            intensity = jnp.zeros((8, EC), jnp.float32)
            for c in range(K2 // 2):
                f0, f1 = fields[c], fields[c + K2 // 2]
                intensity = intensity + gain_ref[c] * (f0 * f0 + f1 * f1)
            resist = sigmoid(STEEP * (intensity - THRESH))
            v = vext[pl.ds(pl.multiple_of(blk * 8, 8), 8), :]
            target = jnp.where(v < 0.0, 1.0, 0.0)
            slopes = (8.0 * jnp.abs(v)) * (resist - target) * resist * (1.0 - resist)
            for c in range(0, K2, 2):
                pair = [2.0 * gain_ref[(c + d) % (K2 // 2)] * fields[c + d] * slopes for d in range(2)]
                gblk[blk, 8 * c : 8 * c + 16, :] = jnp.concatenate(pair, axis=0).astype(jnp.bfloat16)
            return carry

        lax.fori_loop(0, ER // 8, forward, 0)

        def backward(blk, carry):
            window = gblk[pl.ds(blk, 4)].reshape(KB, EC)
            spread = jnp.dot(umat[...], window, preferred_element_type=jnp.float32)
            spread = spread.reshape(JP, 8, EC)
            total = jnp.zeros((8, W), jnp.float32)
            for j in range(KS):
                shift = (EC - (KS - 1 - j)) % EC
                total = total + pltpu.roll(spread[j], shift, 1)[:, :W]
            at = pl.ds(pl.multiple_of(OWN_R + blk * 8, 8), 8)
            gframe[step, at, OWN_C : OWN_C + W] = total
            return carry

        lax.fori_loop(0, H // 8, backward, 0)

        own = gframe.at[step, OWN_R : OWN_R + H, OWN_C : OWN_C + W]
        gradient = own[...] * own_soft * (1.0 - own_soft)
        own[...] = gradient
        if step < ITERS - 1:
            copies_g = frames(own, gframe.at[step], HALO, OWN_R, g_send, g_recv)
            sends += copies_g

        squares = jnp.sum(gradient * gradient, axis=0, keepdims=True)
        squares = squares[:, :128] + squares[:, 128:]

        def reduce(value, at, slots, count, me, device):
            part[at] = value
            slots[step, pl.ds(me, 1)] = value[None]
            for k in range(1, count):
                pltpu.make_async_remote_copy(
                    part.at[at], slots.at[step, me], r_send.at[at], r_recv.at[at], device(k), MESH
                ).start()
            peers = slots.at[step, pl.ds(0, count - 1)]
            every = pltpu.make_async_remote_copy(
                peers, peers, r_send.at[at], r_recv.at[at], device(1), MESH
            )
            every.wait_recv()
            return jnp.sum(slots[step], axis=0), every

        stages = (
            (slots_c, 2, core, other_core),
            (slots_b, nb // 2, b // 2, same_core),
            (slots_w, nw, w, along_work),
        )
        for at, (slots, count, me, device) in enumerate(stages):
            squares, every = reduce(squares, 3 * step + at, slots, count, me, device)
            sends.append(every)
        mean = jnp.sum(squares, axis=1, keepdims=True) * (1.0 / (nb * nw * H * W))
        scale = STEP_SIZE / jnp.sqrt(mean + EPSILON)
        if step < ITERS - 1:
            for copy in copies_g:
                copy.wait_recv()
            frame[...] = frame[...] - scale * gframe[step]
        else:
            out_ref[...] = frame[OWN_R : OWN_R + H, OWN_C : OWN_C + W] - scale * gradient
    for copy in sends:
        copy.wait_send()


def solution(mesh):
    nb, nw = mesh.shape["band"], mesh.shape["work"]

    def shards(mask_logits, loss_weights, target_bits, kernels, kernel_gains, imager_list):
        by_col = jnp.transpose(kernels, (2, 0, 1))
        padded = jnp.pad(by_col, ((0, 1), (0, 0), (0, 7))).reshape(JP, K2, 4, 8)
        fwd = jnp.transpose(padded, (1, 2, 0, 3)).reshape(K2, KF)
        fwd = jnp.pad(fwd, ((0, 0), (0, KFP - KF)))
        flipped = jnp.pad(by_col[:, :, ::-1], ((0, 1), (0, 0), (0, 7))).reshape(JP, K2, 4, 8)
        bwd = jnp.transpose(flipped, (0, 2, 1, 3)).reshape(JP, KB)
        vmem = pl.BlockSpec(memory_space=pltpu.VMEM)
        smem = pl.BlockSpec(memory_space=pltpu.SMEM)
        dma = pltpu.SemaphoreType.DMA
        return pl.pallas_call(
            functools.partial(kernel, nb, nw),
            out_shape=jax.ShapeDtypeStruct((H, W), jnp.float32),
            in_specs=[vmem] * 5 + [smem] * 2,
            out_specs=vmem,
            scratch_shapes=[
                pltpu.VMEM((LR, LC), jnp.float32),
                pltpu.VMEM((ITERS, LR, LC), jnp.float32),
                pltpu.VMEM((H, W), jnp.bfloat16),
                pltpu.VMEM((H + 32, LC), jnp.bfloat16),
                pltpu.VMEM((ER, EC), jnp.float32),
                pltpu.VMEM((K2 * 8, KF), jnp.bfloat16),
                pltpu.VMEM((JP * 8, KB), jnp.bfloat16),
                pltpu.VMEM((LR // 8, JP * 8, EC), jnp.bfloat16),
                pltpu.VMEM((ER // 8, K2 * 8, EC), jnp.bfloat16),
                pltpu.VMEM((ITERS, 2, 1, 128), jnp.float32),
                pltpu.VMEM((ITERS, nb // 2, 1, 128), jnp.float32),
                pltpu.VMEM((ITERS, nw, 1, 128), jnp.float32),
                pltpu.VMEM((3 * ITERS, 1, 128), jnp.float32),
                dma((8,)), dma((8,)), dma((8,)), dma((8,)), dma((8,)), dma((8,)),
                dma((3 * ITERS,)), dma((3 * ITERS,)),
            ],
            compiler_params=pltpu.CompilerParams(
                collective_id=0, has_side_effects=True, vmem_limit_bytes=48 * 1024 * 1024
            ),
        )(
            mask_logits, loss_weights, target_bits, fwd, bwd, kernel_gains, imager_list.reshape(-1)
        )

    in_specs = (
        P("band", "work"),
        P("band", "work"),
        P("band", "work"),
        P(),
        P(),
        P("band", None, None, None),
    )
    return jax.shard_map(
        shards, mesh=mesh, in_specs=in_specs, out_specs=P("band", "work"), check_vma=False
    )
```

time: 534 us -> 64.2 us (0.12)
  blocking collectives: 224 us -> 0 us
  other arithmetic: 89.4 us -> 0 us
  local copies, waits for them, and re-layouts: 92.4 us -> 4.23 us
  matrix products: 61.2 us -> 0 us
  Pallas kernels: 0 us -> 59.7 us
  starting transfers between devices: 38.6 us -> 0 us
  waiting for transfers between devices: 15.5 us -> 0 us
  loops' own time: 9.08 us -> 0 us
    psum x2 -> x0, blocking collectives: 224 us -> none  [shards(): squares_total = lax.psum(jnp.sum(gradient * gradient), ('band', 'work'))]
    another operation x121 -> x0, other arithmetic: 80.9 us -> none
    scatter-add x106 -> x0, local copies, waits for them, and re-layouts: 66.2 us -> none  [the longest x100 65.5 us: image_tile(): mask_grad.at[:, offset_col:offset_col + tile_cols]]
    dot_general x204 -> x0, matrix products: 61.2 us -> none  [the longest x100 36.9 us: image_tile(): jnp.einsum('cd,cyx->dyx', kernels[:, offset_row, :], field_grad, preferre...]
    pallas_call x0 -> x1, Pallas kernels: none -> 59.7 us  [shards(): pl.pallas_call(functools.partial(kernel, nb, nw), out_shape=jax.ShapeDtyp...]
    ppermute x16 -> x0, starting transfers between devices: 38.6 us -> none  [the longest x8 21.1 us: extended(): lax.ppermute(lax.slice_in_dim(block, 0, width, axis=dim), axis, backward)]
    ppermute x16 -> x0, waiting for transfers between devices: 15.5 us -> none  [the longest x8 15.5 us: extended(): lax.ppermute(lax.slice_in_dim(block, 0, width, axis=dim), axis, backward)]
    another operation x124 -> x0, local copies, waits for them, and re-layouts: 14.2 us -> none  [the longest x112 13.2 us: image_tile(): jnp.stack([padded[:, offset_col:offset_col + tile_cols] for offset_col in...]
  transfers between devices with their start and end apart: 16 -> 0, of which waited for: 6 -> 0; matrix products, arithmetic and copies ran while one was open for 2% -> 0% of each run, Pallas kernels for 0% -> 0%
where the time goes in v1:
time: 64.2 us; the launch traced here: 64 us
  Pallas kernels  59.7 us (93%)
  local copies, waits for them, and re-layouts  4.23 us (7%)
    pallas_call x1, Pallas kernels, shards(): pl.pallas_call(functools.partial(kernel, nb, nw), out_shape=jax.ShapeDtyp...  59.7 us
    unnamed x14, local copies, waits for them, and re-layouts  2.55 us

profile of v1, /device:TPU:1, one launch (start us, length us, event | category | flops | bytes accessed | tf_op | source)
XLA Modules:
  0.0 64.0 jit_solution(12935929646403577589)
XLA Ops:
  0.0 0.9 %pad.11 = bf16[26,24,32]{0,1,2:T(8,128)(2,1)S(1)} pad(bf16[25,24,25]{0,1,2:T(8,128)(2,1)} %bitcast.17, bf16[]{:T(256)} %constant.2.clone.1), padding=0_1x0_0x0_7 | pad | bytes 69938 | tf_op jit(solution)/shard_map/jit(_pad)/pad | solution.py:226
  0.9 0.3 copy.10
  1.2 0.0 copy-start.4
  1.3 0.1 copy.11
  1.4 0.8 %copy-done.4 = bf16[24,25,25]{2,0,1:T(8,128)(2,1)S(1)} copy-done((bf16[24,25,25]{2,0,1:T(8,128)(2,1)S(1)}, bf16[24,25,25]{2,0,1:T(8,128)(2,1)}, u32[]{:S(2)}) %copy-start.4) | copy-done | bytes 30024
  2.3 0.0 copy-start.5
  2.3 0.0 copy-start
  2.3 0.0 copy-start.1
  2.3 0.0 copy-start.2
  2.3 0.1 copy.14.kb_ref
  2.5 0.5 copy-done.5
  3.0 0.1 copy.13
  3.0 0.0 copy-start.3
  3.0 0.1 reshape.19.img_ref
  3.1 0.0 copy-done
  3.1 0.0 copy-done.1
  3.1 0.0 copy-done.2
  3.2 0.6 copy-done.3
  3.7 59.7 %shard_map.64 = f32[48,256]{1,0:T(8,128)S(1)} custom-call(f32[48,256]{1,0:T(8,128)S(1)} %copy-done, f32[48,256]{1,0:T(8,128)S(1)} %copy-done.1, s32[48,256]{1,0:T(8,128)S(1)} %copy-done.2, bf16[24,896]{1,0:T(8,128)(2,1)S(1)} %pad.12.kf_ref, bf16[26,768]{1,0:T(8,128)(2,1)S(1)} %copy.14.kb_ref, f32[12]{0:T(128)S(1)} %copy-done.3, s32[32]{0:T(128)S(1)} %reshape.19.img_ref), custom_call_target="tpu_custom_call" | custom-call | tf_op jit(solution)/shard_map/pallas_call | solution.py:234
  63.4 0.6 copy.16
  (4 shorter events, 0.1 us)
Async XLA Ops:
  1.2 0.9 %copy-start.4 = (bf16[24,25,25]{2,0,1:T(8,128)(2,1)S(1)}, bf16[24,25,25]{2,0,1:T(8,128)(2,1)}, u32[]{:S(2)}) copy-start(bf16[24,25,25]{2,0,1:T(8,128)(2,1)} %param.9) | copy-start | bytes 90004
  2.3 0.7 %copy-start.5 = (s32[1,16,2,1]{1,3,2,0:T(1,128)S(1)}, s32[1,16,2,1]{1,3,2,0:T(1,128)}, u32[]{:S(2)}) copy-start(s32[1,16,2,1]{1,3,2,0:T(1,128)} %param.11) | copy-start | bytes 388
  2.3 0.8 %copy-start = (f32[48,256]{1,0:T(8,128)S(1)}, f32[48,256]{1,0:T(8,128)}, u32[]{:S(2)}) copy-start(f32[48,256]{1,0:T(8,128)} %log_ref.1) | copy-start | bytes 147460
  2.3 0.8 %copy-start.1 = (f32[48,256]{1,0:T(8,128)S(1)}, f32[48,256]{1,0:T(8,128)}, u32[]{:S(2)}) copy-start(f32[48,256]{1,0:T(8,128)} %lw_ref.1) | copy-start | bytes 147460
  2.3 0.8 %copy-start.2 = (s32[48,256]{1,0:T(8,128)S(1)}, s32[48,256]{1,0:T(8,128)}, u32[]{:S(2)}) copy-start(s32[48,256]{1,0:T(8,128)} %bits_ref.1) | copy-start | bytes 147460
  3.0 0.7 %copy-start.3 = (f32[12]{0:T(128)S(1)}, f32[12]{0:T(128)}, u32[]{:S(2)}) copy-start(f32[12]{0:T(128)} %gain_ref.1) | copy-start | bytes 148

commit v2 on v1

--- a/solution.py
+++ b/solution.py
@@ -31,7 +31,7 @@
 def kernel(
     nb, nw, log_ref, lw_ref, bits_ref, kf_ref, kb_ref, gain_ref, img_ref, out_ref,
     frame, gframe, vown, vframe, vext, tmat, umat, sblk, gblk, slots_c, slots_b, slots_w, part,
-    a_send, a_recv, v_send, v_recv, g_send, g_recv, r_send, r_recv,
+    a_send, a_recv, v_send, v_recv, g_send, g_recv, r_send, r_recv, knows_four, knows_all,
 ):
     b, w = lax.axis_index("band"), lax.axis_index("work")
     up, down = lax.rem(b + nb - 1, nb), lax.rem(b + 1, nb)
@@ -49,7 +49,9 @@
         return (b, lax.rem(w + k, nw))
 
     barrier = pltpu.get_barrier_semaphore()
-    greeted = [along_work(k) for k in range(1, nw)] + [same_core(k) for k in range(1, nb // 2)]
+    near = [along_work(k) for k in (1, 2, nw - 2, nw - 1)]
+    far = [along_work(k) for k in (3, 4, nw - 4, nw - 3)]
+    greeted = near + [same_core(k) for k in range(1, nb // 2)]
     greeted += [(up, w), (down, w), (up, left), (up, right), (down, left), (down, right)]
     for dev in greeted:
         pl.semaphore_signal(barrier, inc=1, device_id=dev, device_id_type=MESH)
@@ -62,6 +64,8 @@
     vown[...] = jnp.where(bits_ref[...] == 1, -weight, weight).astype(jnp.bfloat16)
 
     pl.semaphore_wait(barrier, len(greeted))
+    for dev in near:
+        pl.semaphore_signal(knows_four, inc=1, device_id=dev, device_id_type=MESH)
 
     def frames(src, dst, h, top, send, recv):
         lo, hi = slice(0, h), slice(H - h, H)
@@ -124,6 +128,9 @@
 
     for copy in copies_a:
         copy.wait_recv()
+    pl.semaphore_wait(knows_four, len(near))
+    for dev in far:
+        pl.semaphore_signal(knows_all, inc=1, device_id=dev, device_id_type=MESH)
 
     band_row = b * H + lax.broadcasted_iota(jnp.int32, (LR, LC), 0) - OWN_R
     band_col = w * W + lax.broadcasted_iota(jnp.int32, (LR, LC), 1) - OWN_C
@@ -141,8 +148,8 @@
             ]
             sblk[:, 8 * j : 8 * j + 16, :] = jnp.concatenate(pair, axis=1).astype(jnp.bfloat16)
 
-        def forward(blk, carry):
-            window = sblk[pl.ds(blk, 4)].reshape(KF, EC)
+        for blk in range(ER // 8):
+            window = sblk[blk : blk + 4].reshape(KF, EC)
             fields = jnp.dot(tmat[...], window, preferred_element_type=jnp.float32)
             fields = fields.reshape(K2, 8, EC)
             intensity = jnp.zeros((8, EC), jnp.float32)
@@ -150,29 +157,23 @@
                 f0, f1 = fields[c], fields[c + K2 // 2]
                 intensity = intensity + gain_ref[c] * (f0 * f0 + f1 * f1)
             resist = sigmoid(STEEP * (intensity - THRESH))
-            v = vext[pl.ds(pl.multiple_of(blk * 8, 8), 8), :]
+            v = vext[8 * blk : 8 * blk + 8, :]
             target = jnp.where(v < 0.0, 1.0, 0.0)
             slopes = (8.0 * jnp.abs(v)) * (resist - target) * resist * (1.0 - resist)
             for c in range(0, K2, 2):
                 pair = [2.0 * gain_ref[(c + d) % (K2 // 2)] * fields[c + d] * slopes for d in range(2)]
                 gblk[blk, 8 * c : 8 * c + 16, :] = jnp.concatenate(pair, axis=0).astype(jnp.bfloat16)
-            return carry
-
-        lax.fori_loop(0, ER // 8, forward, 0)
-
-        def backward(blk, carry):
-            window = gblk[pl.ds(blk, 4)].reshape(KB, EC)
+
+        for blk in range(H // 8):
+            window = gblk[blk : blk + 4].reshape(KB, EC)
             spread = jnp.dot(umat[...], window, preferred_element_type=jnp.float32)
             spread = spread.reshape(JP, 8, EC)
             total = jnp.zeros((8, W), jnp.float32)
             for j in range(KS):
                 shift = (EC - (KS - 1 - j)) % EC
                 total = total + pltpu.roll(spread[j], shift, 1)[:, :W]
-            at = pl.ds(pl.multiple_of(OWN_R + blk * 8, 8), 8)
-            gframe[step, at, OWN_C : OWN_C + W] = total
-            return carry
-
-        lax.fori_loop(0, H // 8, backward, 0)
+            at = OWN_R + blk * 8
+            gframe[step, at : at + 8, OWN_C : OWN_C + W] = total
 
         own = gframe.at[step, OWN_R : OWN_R + H, OWN_C : OWN_C + W]
         gradient = own[...] * own_soft * (1.0 - own_soft)
@@ -204,6 +205,8 @@
             (slots_w, nw, w, along_work),
         )
         for at, (slots, count, me, device) in enumerate(stages):
+            if step == 0 and at == len(stages) - 1:
+                pl.semaphore_wait(knows_all, len(far))
             squares, every = reduce(squares, 3 * step + at, slots, count, me, device)
             sends.append(every)
         mean = jnp.sum(squares, axis=1, keepdims=True) * (1.0 / (nb * nw * H * W))
@@ -252,6 +255,7 @@
                 pltpu.VMEM((3 * ITERS, 1, 128), jnp.float32),
                 dma((8,)), dma((8,)), dma((8,)), dma((8,)), dma((8,)), dma((8,)),
                 dma((3 * ITERS,)), dma((3 * ITERS,)),
+                pltpu.SemaphoreType.REGULAR, pltpu.SemaphoreType.REGULAR,
             ],
             compiler_params=pltpu.CompilerParams(
                 collective_id=0, has_side_effects=True, vmem_limit_bytes=48 * 1024 * 1024

time: 64.2 us -> 55.6 us (0.87)
  Pallas kernels: 59.7 us -> 51 us
    pallas_call x1, Pallas kernels: 59.7 us -> 51 us  [shards(): pl.pallas_call(functools.partial(kernel, nb, nw), out_shape=jax.ShapeDtyp...]
where the time goes in v2:
time: 55.6 us; the launch traced here: 55.4 us
  Pallas kernels  51 us (92%)
  local copies, waits for them, and re-layouts  4.23 us (8%)
    pallas_call x1, Pallas kernels, shards(): pl.pallas_call(functools.partial(kernel, nb, nw), out_shape=jax.ShapeDtyp...  51 us
    unnamed x14, local copies, waits for them, and re-layouts  2.55 us

profile of v2, /device:TPU:1, one launch (start us, length us, event | category | flops | bytes accessed | tf_op | source)
XLA Modules:
  0.0 55.4 jit_solution(18053127145901928348)
XLA Ops:
  0.0 0.9 %pad.11 = bf16[26,24,32]{0,1,2:T(8,128)(2,1)S(1)} pad(bf16[25,24,25]{0,1,2:T(8,128)(2,1)} %bitcast.17, bf16[]{:T(256)} %constant.2.clone.1), padding=0_1x0_0x0_7 | pad | bytes 69938 | tf_op jit(solution)/shard_map/jit(_pad)/pad | solution.py:229
  0.9 0.3 copy.10
  1.2 0.0 copy-start.4
  1.3 0.1 copy.11
  1.4 0.8 %copy-done.4 = bf16[24,25,25]{2,0,1:T(8,128)(2,1)S(1)} copy-done((bf16[24,25,25]{2,0,1:T(8,128)(2,1)S(1)}, bf16[24,25,25]{2,0,1:T(8,128)(2,1)}, u32[]{:S(2)}) %copy-start.4) | copy-done | bytes 30024
  2.3 0.0 copy-start.5
  2.3 0.0 copy-start
  2.3 0.0 copy-start.1
  2.3 0.0 copy-start.2
  2.3 0.1 copy.14.kb_ref
  2.5 0.5 copy-done.5
  3.0 0.1 copy.13
  3.0 0.0 copy-start.3
  3.0 0.1 reshape.19.img_ref
  3.1 0.0 copy-done
  3.1 0.0 copy-done.1
  3.1 0.0 copy-done.2
  3.2 0.6 copy-done.3
  3.7 51.0 %shard_map.64 = f32[48,256]{1,0:T(8,128)S(1)} custom-call(f32[48,256]{1,0:T(8,128)S(1)} %copy-done, f32[48,256]{1,0:T(8,128)S(1)} %copy-done.1, s32[48,256]{1,0:T(8,128)S(1)} %copy-done.2, bf16[24,896]{1,0:T(8,128)(2,1)S(1)} %pad.12.kf_ref, bf16[26,768]{1,0:T(8,128)(2,1)S(1)} %copy.14.kb_ref, f32[12]{0:T(128)S(1)} %copy-done.3, s32[32]{0:T(128)S(1)} %reshape.19.img_ref), custom_call_target="tpu_custom_call" | custom-call | tf_op jit(solution)/shard_map/pallas_call | solution.py:237
  54.8 0.6 %copy.16 = f32[48,256]{1,0:T(8,128)} copy(f32[48,256]{1,0:T(8,128)S(1)} %shard_map.64) | data formatting | bytes 98304
  (4 shorter events, 0.1 us)
Async XLA Ops:
  1.2 0.9 %copy-start.4 = (bf16[24,25,25]{2,0,1:T(8,128)(2,1)S(1)}, bf16[24,25,25]{2,0,1:T(8,128)(2,1)}, u32[]{:S(2)}) copy-start(bf16[24,25,25]{2,0,1:T(8,128)(2,1)} %param.9) | copy-start | bytes 90004
  2.3 0.7 %copy-start.5 = (s32[1,16,2,1]{1,3,2,0:T(1,128)S(1)}, s32[1,16,2,1]{1,3,2,0:T(1,128)}, u32[]{:S(2)}) copy-start(s32[1,16,2,1]{1,3,2,0:T(1,128)} %param.11) | copy-start | bytes 388
  2.3 0.8 %copy-start = (f32[48,256]{1,0:T(8,128)S(1)}, f32[48,256]{1,0:T(8,128)}, u32[]{:S(2)}) copy-start(f32[48,256]{1,0:T(8,128)} %log_ref.1) | copy-start | bytes 147460
  2.3 0.8 %copy-start.1 = (f32[48,256]{1,0:T(8,128)S(1)}, f32[48,256]{1,0:T(8,128)}, u32[]{:S(2)}) copy-start(f32[48,256]{1,0:T(8,128)} %lw_ref.1) | copy-start | bytes 147460
  2.3 0.8 %copy-start.2 = (s32[48,256]{1,0:T(8,128)S(1)}, s32[48,256]{1,0:T(8,128)}, u32[]{:S(2)}) copy-start(s32[48,256]{1,0:T(8,128)} %bits_ref.1) | copy-start | bytes 147460
  3.0 0.7 %copy-start.3 = (f32[12]{0:T(128)S(1)}, f32[12]{0:T(128)}, u32[]{:S(2)}) copy-start(f32[12]{0:T(128)} %gain_ref.1) | copy-start | bytes 148

commit v3 on v2

--- a/solution.py
+++ b/solution.py
@@ -17,9 +17,8 @@
 ER, EC = 72, 384
 LR, LC = 96, 512
 OWN_R, OWN_C = 24, 128
-KF = 4 * JP * 8
-KFP = 896
-KB = 4 * K2 * 8
+QF, QB = 256, 192
+KF, KB = 4 * QF, 4 * QB
 ITERS = 2
 STEEP, THRESH, STEP_SIZE, EPSILON = 4.0, 0.5, 0.5, 1e-6
 
@@ -29,9 +28,11 @@
 
 
 def kernel(
-    nb, nw, log_ref, lw_ref, bits_ref, kf_ref, kb_ref, gain_ref, img_ref, out_ref,
-    frame, gframe, vown, vframe, vext, tmat, umat, sblk, gblk, slots_c, slots_b, slots_w, part,
-    a_send, a_recv, v_send, v_recv, g_send, g_recv, r_send, r_recv, knows_four, knows_all,
+    nb, nw, log_hbm, lw_hbm, bits_hbm, kern_hbm, gain_hbm, img_hbm, out_ref,
+    log_ref, lw_ref, bits_ref, kern_ref, gain_ref, img_ref,
+    frame, gframe, vown, vframe, vext, wide, tmat, umat, sblk, gblk,
+    slots_c, slots_b, slots_w, part,
+    l_sem, a_send, a_recv, v_send, v_recv, g_send, g_recv, r_send, r_recv, knows_four, knows_all,
 ):
     b, w = lax.axis_index("band"), lax.axis_index("work")
     up, down = lax.rem(b + nb - 1, nb), lax.rem(b + 1, nb)
@@ -56,9 +57,20 @@
     for dev in greeted:
         pl.semaphore_signal(barrier, inc=1, device_id=dev, device_id_type=MESH)
 
+    pairs = (
+        (lw_hbm, lw_ref), (bits_hbm, bits_ref), (img_hbm, img_ref),
+        (log_hbm, log_ref), (kern_hbm, kern_ref), (gain_hbm, gain_ref),
+    )
+    loads = [pltpu.make_async_copy(src, dst, l_sem.at[k]) for k, (src, dst) in enumerate(pairs)]
+    for load in loads:
+        load.start()
+    sblk[:, 8 * JP :, :] = jnp.zeros((LR // 8, QF - 8 * JP, EC), jnp.bfloat16)
+    for load in loads[:3]:
+        load.wait()
+
     rows = lax.broadcasted_iota(jnp.int32, (H, W), 0)
-    live0 = jnp.where(img_ref[w * 2] < nw, 1.0, 0.0)
-    live1 = jnp.where(img_ref[w * 2 + 1] < nw, 1.0, 0.0)
+    live0 = jnp.where(img_ref[0, 0, 0, w] < nw, 1.0, 0.0)
+    live1 = jnp.where(img_ref[0, 1, 0, w] < nw, 1.0, 0.0)
     weight = lw_ref[...].astype(jnp.bfloat16).astype(jnp.float32)
     weight = weight * jnp.where(rows < TR, live0, live1)
     vown[...] = jnp.where(bits_ref[...] == 1, -weight, weight).astype(jnp.bfloat16)
@@ -94,28 +106,34 @@
             copy.start()
         return copies
 
+    loads[3].wait()
     copies_v = frames(vown, vframe, 16, 16, v_send, v_recv)
     copies_a = frames(log_ref, frame, HALO, OWN_R, a_send, a_recv)
     frame[OWN_R : OWN_R + H, OWN_C : OWN_C + W] = log_ref[...]
     vframe[16 : 16 + H, 128 : 128 + W] = vown[...]
 
-    lane_f = lax.broadcasted_iota(jnp.int32, (8, KFP), 1) & 7
-    sub_f = lax.broadcasted_iota(jnp.int32, (8, KFP), 0)
-    lane_b = lax.broadcasted_iota(jnp.int32, (8, KB), 1) & 7
-    sub_b = lax.broadcasted_iota(jnp.int32, (8, KB), 0)
-
-    def toeplitz(row, lane, sub, step):
-        wide = jnp.broadcast_to(row.astype(jnp.float32), lane.shape)
-        same = pltpu.roll(wide, 0, 1, stride=1, stride_axis=0)
-        prior = pltpu.roll(wide, step - 8, 1, stride=1, stride_axis=0)
-        return jnp.where(lane >= sub, same, prior)
-
-    for c in range(0, K2, 2):
-        pair = [toeplitz(kf_ref[c + d : c + d + 1, :], lane_f, sub_f, JP * 8) for d in range(2)]
-        tmat[8 * c : 8 * c + 16, :] = jnp.concatenate(pair, axis=0)[:, :KF].astype(jnp.bfloat16)
-    for j in range(0, JP, 2):
-        pair = [toeplitz(kb_ref[j + d : j + d + 1, :], lane_b, sub_b, K2 * 8) for d in range(2)]
-        umat[8 * j : 8 * j + 16, :] = jnp.concatenate(pair, axis=0).astype(jnp.bfloat16)
+    for load in loads[4:]:
+        load.wait()
+    taps = jnp.transpose(kern_ref[...].astype(jnp.float32).reshape(KS * K2, KS)).astype(jnp.bfloat16)
+    lane = lax.broadcasted_iota(jnp.int32, (1, KF), 1)
+    channel = (lane >> 3) & 31
+    tap = KS - 1 - 8 * (lane >> 8) - (lane & 7)
+    source = jnp.where((channel < K2) & (tap >= 0), tap * K2 + channel, -1)
+    chosen = lax.broadcasted_iota(jnp.int32, (KS * K2, KF), 0) == source
+    chosen = jnp.where(chosen, 1.0, 0.0).astype(jnp.bfloat16)
+    base = jnp.dot(taps, chosen, preferred_element_type=jnp.float32)
+    lane8 = lax.broadcasted_iota(jnp.int32, (8, KF), 1) & 7
+    sub = lax.broadcasted_iota(jnp.int32, (8, KF), 0)
+    for j in range(KS):
+        row = jnp.broadcast_to(base[j : j + 1, :], (8, KF))
+        same = pltpu.roll(row, 0, 1, stride=1, stride_axis=0)
+        prior = pltpu.roll(row, QF - 8, 1, stride=1, stride_axis=0)
+        wide[8 * j : 8 * j + 8, :] = jnp.where(lane8 >= sub, same, prior)
+    wide[8 * KS :, :] = jnp.zeros((QF - 8 * KS, KF), jnp.float32)
+    for q in range(4):
+        umat[:, QB * q : QB * q + QB] = wide[: 8 * JP, QF * q : QF * q + QB].astype(jnp.bfloat16)
+        turned = jnp.transpose(wide[:, QF * (3 - q) : QF * (4 - q)])
+        tmat[:, QF * q : QF * q + QF] = turned[:QB].astype(jnp.bfloat16)
 
     for copy in copies_v:
         copy.wait_recv()
@@ -225,43 +243,49 @@
     nb, nw = mesh.shape["band"], mesh.shape["work"]
 
     def shards(mask_logits, loss_weights, target_bits, kernels, kernel_gains, imager_list):
-        by_col = jnp.transpose(kernels, (2, 0, 1))
-        padded = jnp.pad(by_col, ((0, 1), (0, 0), (0, 7))).reshape(JP, K2, 4, 8)
-        fwd = jnp.transpose(padded, (1, 2, 0, 3)).reshape(K2, KF)
-        fwd = jnp.pad(fwd, ((0, 0), (0, KFP - KF)))
-        flipped = jnp.pad(by_col[:, :, ::-1], ((0, 1), (0, 0), (0, 7))).reshape(JP, K2, 4, 8)
-        bwd = jnp.transpose(flipped, (0, 2, 1, 3)).reshape(JP, KB)
         vmem = pl.BlockSpec(memory_space=pltpu.VMEM)
-        smem = pl.BlockSpec(memory_space=pltpu.SMEM)
+        hbm = pl.BlockSpec(memory_space=pltpu.HBM)
         dma = pltpu.SemaphoreType.DMA
         return pl.pallas_call(
             functools.partial(kernel, nb, nw),
             out_shape=jax.ShapeDtypeStruct((H, W), jnp.float32),
-            in_specs=[vmem] * 5 + [smem] * 2,
+            in_specs=[hbm] * 6,
             out_specs=vmem,
             scratch_shapes=[
+                pltpu.VMEM((H, W), jnp.float32),
+                pltpu.VMEM((H, W), jnp.float32),
+                pltpu.VMEM((H, W), jnp.int32),
+                pltpu.VMEM((KS, K2, KS), jnp.bfloat16),
+                pltpu.SMEM((K2 // 2,), jnp.float32),
+                pltpu.SMEM((1, H // TR, 1, nw), jnp.int32),
                 pltpu.VMEM((LR, LC), jnp.float32),
                 pltpu.VMEM((ITERS, LR, LC), jnp.float32),
                 pltpu.VMEM((H, W), jnp.bfloat16),
                 pltpu.VMEM((H + 32, LC), jnp.bfloat16),
                 pltpu.VMEM((ER, EC), jnp.float32),
-                pltpu.VMEM((K2 * 8, KF), jnp.bfloat16),
+                pltpu.VMEM((QF, KF), jnp.float32),
+                pltpu.VMEM((QB, KF), jnp.bfloat16),
                 pltpu.VMEM((JP * 8, KB), jnp.bfloat16),
-                pltpu.VMEM((LR // 8, JP * 8, EC), jnp.bfloat16),
-                pltpu.VMEM((ER // 8, K2 * 8, EC), jnp.bfloat16),
+                pltpu.VMEM((LR // 8, QF, EC), jnp.bfloat16),
+                pltpu.VMEM((ER // 8, QB, EC), jnp.bfloat16),
                 pltpu.VMEM((ITERS, 2, 1, 128), jnp.float32),
                 pltpu.VMEM((ITERS, nb // 2, 1, 128), jnp.float32),
                 pltpu.VMEM((ITERS, nw, 1, 128), jnp.float32),
                 pltpu.VMEM((3 * ITERS, 1, 128), jnp.float32),
-                dma((8,)), dma((8,)), dma((8,)), dma((8,)), dma((8,)), dma((8,)),
+                dma((6,)), dma((8,)), dma((8,)), dma((8,)), dma((8,)), dma((8,)), dma((8,)),
                 dma((3 * ITERS,)), dma((3 * ITERS,)),
                 pltpu.SemaphoreType.REGULAR, pltpu.SemaphoreType.REGULAR,
             ],
             compiler_params=pltpu.CompilerParams(
-                collective_id=0, has_side_effects=True, vmem_limit_bytes=48 * 1024 * 1024
+                collective_id=0, has_side_effects=True, vmem_limit_bytes=62 * 1024 * 1024
             ),
         )(
-            mask_logits, loss_weights, target_bits, fwd, bwd, kernel_gains, imager_list.reshape(-1)
+            mask_logits,
+            loss_weights,
+            target_bits,
+            jnp.transpose(kernels, (1, 0, 2)),
+            kernel_gains,
+            jnp.transpose(imager_list, (0, 2, 3, 1)),
         )
 
     in_specs = (

time: 55.6 us -> 52.9 us (0.951)
  local copies, waits for them, and re-layouts: 4.23 us -> 1.42 us
    unnamed x14 -> x1, local copies, waits for them, and re-layouts: 2.55 us -> 1.42 us
    pad x3 -> x0, local copies, waits for them, and re-layouts: 0.99 us -> none  [the longest x1 0.95 us: shards(): padded = jnp.pad(by_col, ((0, 1), (0, 0), (0, 7))).reshape(JP, K2, 4, 8)]
    reshape x5 -> x0, local copies, waits for them, and re-layouts: 0.67 us -> none  [the longest x1 0.3 us: shards(): padded = jnp.pad(by_col, ((0, 1), (0, 0), (0, 7))).reshape(JP, K2, 4, 8)]
where the time goes in v3:
time: 52.9 us; the launch traced here: 52.8 us
  Pallas kernels  51.3 us (97%)
  local copies, waits for them, and re-layouts  1.42 us (3%)
    pallas_call x1, Pallas kernels, shards(): pl.pallas_call(functools.partial(kernel, nb, nw), out_shape=jax.ShapeDtyp...  51.3 us
    unnamed x1, local copies, waits for them, and re-layouts  1.42 us

profile of v3, /device:TPU:1, one launch (start us, length us, event | category | flops | bytes accessed | tf_op | source)
XLA Modules:
  0.0 52.8 jit_solution(12099919756383894584)
XLA Ops:
  0.0 51.3 %shard_map.64 = f32[48,256]{1,0:T(8,128)} custom-call(f32[48,256]{1,0:T(8,128)} %log_hbm.1, f32[48,256]{1,0:T(8,128)} %lw_hbm.1, s32[48,256]{1,0:T(8,128)} %bits_hbm.1, bf16[25,24,25]{2,1,0:T(8,128)(2,1)} %bitcast.2, f32[12]{0:T(128)} %gain_hbm.1, s32[1,2,1,16]{3,2,1,0:T(1,128)} %bitcast.3), custom_call_target="tpu_custom_call" | custom-call | tf_op jit(solution)/shard_map/pallas_call | solution.py:249
  51.3 1.4 %copy.8 = f32[48,256]{1,0:T(8,128)} copy(f32[48,256]{1,0:T(8,128)} %shard_map.64) | data formatting | bytes 98304

commit v4 on v3

v4 whole, which is shorter than its diff:
```python
import functools

import jax
import jax.numpy as jnp
from jax import lax
from jax.experimental import pallas as pl
from jax.experimental.pallas import tpu as pltpu
from jax.sharding import PartitionSpec as P

MESH = pl.DeviceIdType.MESH
TR = 24
H, W = 48, 256
K2 = 24
KS = 25
JP = 26
HALO = 24
ER, EC = 72, 256
XC = 24
SLOT, XL, XG = 48, 512, 384
XAT = 104 + EC
LR, LC = 96, 512
OWN_R, OWN_C = 24, 128
QF, QB = 256, 192
KF, KB = 4 * QF, 4 * QB
ITERS = 2
STEEP, THRESH, STEP_SIZE, EPSILON = 4.0, 0.5, 0.5, 1e-6


def farthest_first(*rings):
    count = 1
    for ring in rings:
        count *= ring

    def links(k):
        total = 0
        for ring in reversed(rings):
            total += min(k % ring, ring - k % ring)
            k //= ring
        return total

    return sorted(range(1, count), key=lambda k: -links(k))


def sigmoid(x):
    return 1.0 / (1.0 + jnp.exp(-x))


def kernel(
    nb, nw, log_hbm, lw_hbm, bits_hbm, kern_hbm, gain_hbm, img_hbm, out_ref,
    lw_ref, bits_ref, kern_ref, gain_ref, img_ref,
    both, frame, gframe, vext, vlast, mlast, wide, tmat, umat, sblk, sxblk, gblk, gxblk,
    slots_c, slots_b, slots_w, part,
    l_sem, a_send, a_recv, g_send, g_recv, r_send, r_recv, knows_four, knows_all,
):
    b, w = lax.axis_index("band"), lax.axis_index("work")
    up, down = lax.rem(b + nb - 1, nb), lax.rem(b + 1, nb)
    left, right = lax.rem(w + nw - 1, nw), lax.rem(w + 1, nw)

    core = lax.rem(b, 2)

    def other_core(k):
        return (b + 1 - 2 * core, w)

    def same_core(k):
        return (lax.rem(b + 2 * k, nb), w)

    def along_work(k):
        return (b, lax.rem(w + k, nw))

    barrier = pltpu.get_barrier_semaphore()
    near = [along_work(k) for k in (1, 2, nw - 2, nw - 1)]
    far = [along_work(k) for k in (3, 4, nw - 4, nw - 3)]
    greeted = [(up, left), (up, right), (down, left), (down, right), (up, w), (down, w)]
    greeted += near + [same_core(k) for k in range(1, nb // 2)]
    for dev in greeted:
        pl.semaphore_signal(barrier, inc=1, device_id=dev, device_id_type=MESH)

    pairs = (
        (lw_hbm, lw_ref), (bits_hbm, bits_ref), (img_hbm, img_ref),
        (log_hbm, both.at[0]), (kern_hbm, kern_ref), (gain_hbm, gain_ref),
    )
    loads = [pltpu.make_async_copy(src, dst, l_sem.at[k]) for k, (src, dst) in enumerate(pairs)]
    for load in loads:
        load.start()
    sblk[:, 8 * JP :, :] = jnp.zeros((LR // 8, QF - 8 * JP, EC), jnp.bfloat16)
    for q in range(4):
        sxblk[QF * q + 8 * JP : QF * q + QF, :] = jnp.zeros((QF - 8 * JP, XL), jnp.bfloat16)
    for load in loads[:3]:
        load.wait()

    rows = lax.broadcasted_iota(jnp.int32, (H, W), 0)
    live0 = jnp.where(img_ref[0, 0, 0, w] < nw, 1.0, 0.0)
    live1 = jnp.where(img_ref[0, 1, 0, w] < nw, 1.0, 0.0)
    weight = lw_ref[...].astype(jnp.bfloat16).astype(jnp.float32)
    weight = weight * jnp.where(rows < TR, live0, live1)
    both[1] = jnp.where(bits_ref[...] == 1, -weight, weight)

    pl.semaphore_wait(barrier, len(greeted))
    for dev in near:
        pl.semaphore_signal(knows_four, inc=1, device_id=dev, device_id_type=MESH)

    def rims(src, dst, send, recv):
        every = slice(None)
        lo, hi = slice(0, HALO), slice(H - HALO, H)
        first, last = slice(0, 128), slice(W - 128, W)
        above, below, mid = slice(0, OWN_R), slice(OWN_R + H, LR), slice(OWN_R, OWN_R + H)
        before, after, centre = slice(0, OWN_C), slice(OWN_C + W, LC), slice(OWN_C, OWN_C + W)
        plan = (
            (lo, first, below, after, (up, left)),
            (lo, last, below, before, (up, right)),
            (hi, first, above, after, (down, left)),
            (hi, last, above, before, (down, right)),
            (lo, slice(0, W), below, centre, (up, w)),
            (hi, slice(0, W), above, centre, (down, w)),
            (slice(0, H), first, mid, after, (b, left)),
            (slice(0, H), last, mid, before, (b, right)),
        )
        copies = []
        for k, (sr, sc, dr, dc, dev) in enumerate(plan):
            copies.append(
                pltpu.make_async_remote_copy(
                    src.at[every, sr, sc], dst.at[every, dr, dc], send.at[k], recv.at[k], dev, MESH
                )
            )
        for copy in copies:
            copy.start()
        return copies

    loads[3].wait()
    copies_a = rims(both, frame, a_send, a_recv)
    frame[:, OWN_R : OWN_R + H, OWN_C : OWN_C + W] = both[...]

    for load in loads[4:]:
        load.wait()
    taps = jnp.transpose(kern_ref[...].astype(jnp.float32).reshape(KS * K2, KS)).astype(jnp.bfloat16)
    lane = lax.broadcasted_iota(jnp.int32, (1, KF), 1)
    channel = (lane >> 3) & 31
    tap = KS - 1 - 8 * (lane >> 8) - (lane & 7)
    source = jnp.where((channel < K2) & (tap >= 0), tap * K2 + channel, -1)
    chosen = lax.broadcasted_iota(jnp.int32, (KS * K2, KF), 0) == source
    chosen = jnp.where(chosen, 1.0, 0.0).astype(jnp.bfloat16)
    base = jnp.dot(taps, chosen, preferred_element_type=jnp.float32)
    lane8 = lax.broadcasted_iota(jnp.int32, (8, KF), 1) & 7
    sub = lax.broadcasted_iota(jnp.int32, (8, KF), 0)
    for j in range(KS):
        row = jnp.broadcast_to(base[j : j + 1, :], (8, KF))
        same = pltpu.roll(row, 0, 1, stride=1, stride_axis=0)
        prior = pltpu.roll(row, QF - 8, 1, stride=1, stride_axis=0)
        wide[8 * j : 8 * j + 8, :] = jnp.where(lane8 >= sub, same, prior)
    wide[8 * KS :, :] = jnp.zeros((QF - 8 * KS, KF), jnp.float32)
    for q in range(4):
        umat[:, QB * q : QB * q + QB] = wide[: 8 * JP, QF * q : QF * q + QB].astype(jnp.bfloat16)
        turned = jnp.transpose(wide[:, QF * (3 - q) : QF * (4 - q)])
        tmat[:, QF * q : QF * q + QF] = turned[:QB].astype(jnp.bfloat16)

    def weights(low, high):
        shape = (high - low, LC)
        band_row = b * H + lax.broadcasted_iota(jnp.int32, shape, 0) + (low - 12)
        band_col = w * W + lax.broadcasted_iota(jnp.int32, shape, 1) - OWN_C
        inside = (band_row >= 0) & (band_row < nb * H) & (band_col >= 0) & (band_col < nw * W)
        signed = jnp.where(inside, frame[1, 12 + low : 12 + high, :], 0.0)
        signed = pltpu.roll(signed, LC - 116, 1)
        vext[low:high, :] = signed[:, :EC]
        vlast[low:high, :] = jnp.where(slot_lane[:, :128] < XC, signed[:, EC : EC + 128], 0.0)

    slot_lane = lax.broadcasted_iota(jnp.int32, (1, LC), 1)
    band_col = w * W + lax.broadcasted_iota(jnp.int32, (8, LC), 1) - OWN_C
    middle = jnp.where((band_col >= 0) & (band_col < nw * W), 1.0, 0.0)
    upper, lower = jnp.where(b > 0, middle, 0.0), jnp.where(b < nb - 1, middle, 0.0)

    sends = list(copies_a)
    for step in range(ITERS):
        def shifted(blk):
            inside = upper if blk < 3 else middle if blk < 9 else lower
            soft = sigmoid(frame[0, 8 * blk : 8 * blk + 8, :])
            rows8 = soft.astype(jnp.bfloat16).astype(jnp.float32) * inside
            last = pltpu.roll(rows8, LC - XAT, 1)[:, :128]
            mlast[8 * blk : 8 * blk + 8, :] = jnp.where(slot_lane[:, :128] < SLOT, last, 0.0)
            rows8 = rows8[:, :XG]
            for j in range(0, JP, 2):
                pair = [pltpu.roll(rows8, XG - 104 - min(j + d, KS - 1), 1)[:, :EC] for d in range(2)]
                sblk[blk, 8 * j : 8 * j + 16, :] = jnp.concatenate(pair, axis=0).astype(jnp.bfloat16)

        def side_by_side(ref, height):
            total = None
            for blk in range(ER // 8):
                part = ref[8 * blk : 8 * blk + height, :]
                part = jnp.concatenate([part, jnp.zeros((height, XL - 128), jnp.float32)], axis=1)
                part = pltpu.roll(part, SLOT * blk, 1) if blk else part
                total = part if total is None else total + part
            return total

        def shifted_last():
            rows32 = side_by_side(mlast, 32)
            for j in range(0, JP, 2):
                pair = []
                for d in range(2):
                    shift = min(j + d, KS - 1)
                    pair.append(pltpu.roll(rows32, XL - shift, 1) if shift else rows32)
                for q in range(4):
                    both8 = [p[8 * q : 8 * q + 8] for p in pair]
                    at = QF * q + 8 * j
                    sxblk[at : at + 16, :] = jnp.concatenate(both8, axis=0).astype(jnp.bfloat16)

        def field_gradient(fields, v, store):
            lanes = v.shape[1]
            fields = fields.reshape(K2, 8, lanes)
            intensity = jnp.zeros((8, lanes), jnp.float32)
            for c in range(K2 // 2):
                f0, f1 = fields[c], fields[c + K2 // 2]
                intensity = intensity + gain_ref[c] * (f0 * f0 + f1 * f1)
            resist = sigmoid(STEEP * (intensity - THRESH))
            target = jnp.where(v < 0.0, 1.0, 0.0)
            slopes = (8.0 * jnp.abs(v)) * (resist - target) * resist * (1.0 - resist)
            for c in range(0, K2, 2):
                pair = [2.0 * gain_ref[(c + d) % (K2 // 2)] * fields[c + d] * slopes for d in range(2)]
                store(8 * c, jnp.concatenate(pair, axis=0))

        def forward(blk):
            window = sblk[blk : blk + 4].reshape(KF, EC)
            fields = jnp.dot(tmat[...], window, preferred_element_type=jnp.float32)

            def store(at, value):
                gblk[blk, at : at + 16, :] = value.astype(jnp.bfloat16)

            field_gradient(fields, vext[8 * blk : 8 * blk + 8, :], store)

        def forward_last():
            fields = jnp.dot(tmat[...], sxblk[...], preferred_element_type=jnp.float32)

            def store(at, value):
                for q in range(4):
                    moved = pltpu.roll(value, XL - SLOT * q, 1) if q else value
                    if XL - SLOT * q < XG:
                        moved = jnp.where(slot_lane < XL - SLOT * q, moved, 0.0)
                    gxblk[QB * q + at : QB * q + at + 16, :] = moved[:, :XG].astype(jnp.bfloat16)

            field_gradient(fields, side_by_side(vlast, 8), store)

        def backward_last():
            spread = jnp.dot(umat[...], gxblk[...], preferred_element_type=jnp.float32)
            spread = spread.reshape(JP, 8, XG)
            total = spread[0]
            for j in range(1, KS):
                total = total + pltpu.roll(spread[j], j, 1)
            lane = lax.broadcasted_iota(jnp.int32, (8, W), 1)
            parts = [pltpu.roll(total, (W - XC - SLOT * k) % XG, 1)[:, :W] for k in range(H // 8)]
            return jnp.concatenate([jnp.where(lane >= W - XC, p, 0.0) for p in parts], axis=0)

        def backward(blk):
            window = gblk[blk : blk + 4].reshape(KB, EC)
            spread = jnp.dot(umat[...], window, preferred_element_type=jnp.float32)
            spread = spread.reshape(JP, 8, EC)
            lane = lax.broadcasted_iota(jnp.int32, (8, EC), 1)
            total = jnp.zeros((8, W), jnp.float32)
            for j in range(KS):
                shift = KS - 1 - j
                moved = pltpu.roll(spread[j], EC - shift, 1) if shift else spread[j]
                total = total + jnp.where(lane < W - shift, moved, 0.0)
            at = OWN_R + blk * 8
            gframe[step, at : at + 8, OWN_C : OWN_C + W] = total

        if step == 0:
            for copy in copies_a[6:]:
                copy.wait_recv()
            weights(24, 48)
        for blk in range(3, 9):
            shifted(blk)
        for blk in range(3, 6):
            forward(blk)
        if step == 0:
            for copy in copies_a[:6]:
                copy.wait_recv()
            pl.semaphore_wait(knows_four, len(near))
            for dev in far:
                pl.semaphore_signal(knows_all, inc=1, device_id=dev, device_id_type=MESH)
            weights(0, 24)
            weights(48, 72)
        for blk in (0, 1, 2):
            shifted(blk)
        for blk in (0, 1, 2):
            forward(blk)
        for blk in (9, 10, 11):
            shifted(blk)
        shifted_last()
        forward_last()
        for blk in (6, 7, 8):
            forward(blk)
        for blk in (0, 1, 2):
            backward(blk)
        last = backward_last()
        for blk in (3, 4, 5):
            backward(blk)

        own = gframe.at[step, OWN_R : OWN_R + H, OWN_C : OWN_C + W]
        own_soft = sigmoid(frame[0, OWN_R : OWN_R + H, OWN_C : OWN_C + W])
        gradient = (own[...] + last) * own_soft * (1.0 - own_soft)
        own[...] = gradient
        if step < ITERS - 1:
            copies_g = rims(gframe.at[pl.ds(step, 1), OWN_R : OWN_R + H, OWN_C : OWN_C + W], gframe.at[pl.ds(step, 1)], g_send, g_recv)
            sends += copies_g

        squares = jnp.sum(gradient * gradient, axis=0, keepdims=True)
        squares = squares[:, :128] + squares[:, 128:]

        def reduce(value, at, slots, order, me, device):
            count = len(order) + 1
            part[at] = value
            slots[step, pl.ds(me, 1)] = value[None]
            for k in order:
                pltpu.make_async_remote_copy(
                    part.at[at], slots.at[step, me], r_send.at[at], r_recv.at[at], device(k), MESH
                ).start()
            peers = slots.at[step, pl.ds(0, count - 1)]
            every = pltpu.make_async_remote_copy(
                peers, peers, r_send.at[at], r_recv.at[at], device(1), MESH
            )
            every.wait_recv()
            return jnp.sum(slots[step], axis=0), every

        stages = (
            (slots_c, [1], core, other_core),
            (slots_b, farthest_first(nb // 8, 4), b // 2, same_core),
            (slots_w, farthest_first(nw), w, along_work),
        )
        for at, (slots, order, me, device) in enumerate(stages):
            if step == 0 and at == len(stages) - 1:
                pl.semaphore_wait(knows_all, len(far))
            squares, every = reduce(squares, 3 * step + at, slots, order, me, device)
            sends.append(every)
        mean = jnp.sum(squares, axis=1, keepdims=True) * (1.0 / (nb * nw * H * W))
        scale = STEP_SIZE / jnp.sqrt(mean + EPSILON)
        if step < ITERS - 1:
            for copy in copies_g:
                copy.wait_recv()
            frame[0] = frame[0] - scale * gframe[step]
        else:
            out_ref[...] = frame[0, OWN_R : OWN_R + H, OWN_C : OWN_C + W] - scale * gradient
    for copy in sends:
        copy.wait_send()


def solution(mesh):
    nb, nw = mesh.shape["band"], mesh.shape["work"]

    def shards(mask_logits, loss_weights, target_bits, kernels, kernel_gains, imager_list):
        vmem = pl.BlockSpec(memory_space=pltpu.VMEM)
        hbm = pl.BlockSpec(memory_space=pltpu.HBM)
        dma = pltpu.SemaphoreType.DMA
        return pl.pallas_call(
            functools.partial(kernel, nb, nw),
            out_shape=jax.ShapeDtypeStruct((H, W), jnp.float32),
            in_specs=[hbm] * 6,
            out_specs=vmem,
            scratch_shapes=[
                pltpu.VMEM((H, W), jnp.float32),
                pltpu.VMEM((H, W), jnp.int32),
                pltpu.VMEM((KS, K2, KS), jnp.bfloat16),
                pltpu.SMEM((K2 // 2,), jnp.float32),
                pltpu.SMEM((1, H // TR, 1, nw), jnp.int32),
                pltpu.VMEM((2, H, W), jnp.float32),
                pltpu.VMEM((2, LR, LC), jnp.float32),
                pltpu.VMEM((ITERS, LR, LC), jnp.float32),
                pltpu.VMEM((ER, EC), jnp.float32),
                pltpu.VMEM((ER, 128), jnp.float32),
                pltpu.VMEM((LR, 128), jnp.float32),
                pltpu.VMEM((QF, KF), jnp.float32),
                pltpu.VMEM((QB, KF), jnp.bfloat16),
                pltpu.VMEM((JP * 8, KB), jnp.bfloat16),
                pltpu.VMEM((LR // 8, QF, EC), jnp.bfloat16),
                pltpu.VMEM((KF, XL), jnp.bfloat16),
                pltpu.VMEM((ER // 8, QB, EC), jnp.bfloat16),
                pltpu.VMEM((KB, XG), jnp.bfloat16),
                pltpu.VMEM((ITERS, 2, 1, 128), jnp.float32),
                pltpu.VMEM((ITERS, nb // 2, 1, 128), jnp.float32),
                pltpu.VMEM((ITERS, nw, 1, 128), jnp.float32),
                pltpu.VMEM((3 * ITERS, 1, 128), jnp.float32),
                dma((6,)), dma((8,)), dma((8,)), dma((8,)), dma((8,)),
                dma((3 * ITERS,)), dma((3 * ITERS,)),
                pltpu.SemaphoreType.REGULAR, pltpu.SemaphoreType.REGULAR,
            ],
            compiler_params=pltpu.CompilerParams(
                collective_id=0, has_side_effects=True, vmem_limit_bytes=62 * 1024 * 1024
            ),
        )(
            mask_logits,
            loss_weights,
            target_bits,
            jnp.transpose(kernels, (1, 0, 2)),
            kernel_gains,
            jnp.transpose(imager_list, (0, 2, 3, 1)),
        )

    in_specs = (
        P("band", "work"),
        P("band", "work"),
        P("band", "work"),
        P(),
        P(),
        P("band", None, None, None),
    )
    return jax.shard_map(
        shards, mesh=mesh, in_specs=in_specs, out_specs=P("band", "work"), check_vma=False
    )
```

time: 52.9 us -> 50.5 us (0.955)
  Pallas kernels: 51.3 us -> 48.9 us
    pallas_call x1, Pallas kernels: 51.3 us -> 48.9 us  [shards(): pl.pallas_call(functools.partial(kernel, nb, nw), out_shape=jax.ShapeDtyp...]
where the time goes in v4:
time: 50.5 us; the launch traced here: 50.3 us
  Pallas kernels  48.9 us (97%)
  local copies, waits for them, and re-layouts  1.42 us (3%)
    pallas_call x1, Pallas kernels, shards(): pl.pallas_call(functools.partial(kernel, nb, nw), out_shape=jax.ShapeDtyp...  48.9 us
    unnamed x1, local copies, waits for them, and re-layouts  1.42 us

profile of v4, /device:TPU:1, one launch (start us, length us, event | category | flops | bytes accessed | tf_op | source)
XLA Modules:
  0.0 50.3 jit_solution(7490757409102768122)
XLA Ops:
  0.0 48.9 %shard_map.64 = f32[48,256]{1,0:T(8,128)} custom-call(f32[48,256]{1,0:T(8,128)} %log_hbm.1, f32[48,256]{1,0:T(8,128)} %lw_hbm.1, s32[48,256]{1,0:T(8,128)} %bits_hbm.1, bf16[25,24,25]{2,1,0:T(8,128)(2,1)} %bitcast.2, f32[12]{0:T(128)} %gain_hbm.1, s32[1,2,1,16]{3,2,1,0:T(1,128)} %bitcast.3), custom_call_target="tpu_custom_call" | custom-call | tf_op jit(solution)/shard_map/pallas_call | solution.py:350
  48.9 1.4 %copy.8 = f32[48,256]{1,0:T(8,128)} copy(f32[48,256]{1,0:T(8,128)} %shard_map.64) | data formatting | bytes 98304

commit v5 on v4

--- a/solution.py
+++ b/solution.py
@@ -344,6 +344,14 @@
     nb, nw = mesh.shape["band"], mesh.shape["work"]
 
     def shards(mask_logits, loss_weights, target_bits, kernels, kernel_gains, imager_list):
+        operands = (
+            mask_logits,
+            loss_weights,
+            target_bits,
+            jnp.transpose(kernels, (1, 0, 2)),
+            kernel_gains,
+            jnp.transpose(imager_list, (0, 2, 3, 1)),
+        )
         vmem = pl.BlockSpec(memory_space=pltpu.VMEM)
         hbm = pl.BlockSpec(memory_space=pltpu.HBM)
         dma = pltpu.SemaphoreType.DMA
@@ -380,15 +388,10 @@
                 pltpu.SemaphoreType.REGULAR, pltpu.SemaphoreType.REGULAR,
             ],
             compiler_params=pltpu.CompilerParams(
-                collective_id=0, has_side_effects=True, vmem_limit_bytes=62 * 1024 * 1024
+                collective_id=0, has_side_effects=True, vmem_limit_bytes=40 * 1024 * 1024
             ),
         )(
-            mask_logits,
-            loss_weights,
-            target_bits,
-            jnp.transpose(kernels, (1, 0, 2)),
-            kernel_gains,
-            jnp.transpose(imager_list, (0, 2, 3, 1)),
+            *[pltpu.with_memory_space_constraint(operand, pltpu.HBM) for operand in operands]
         )
 
     in_specs = (

time: 50.5 us -> 49 us (0.970)
  local copies, waits for them, and re-layouts: 1.42 us -> 0.62 us
  Pallas kernels: 48.9 us -> 48.3 us
    unnamed x1, local copies, waits for them, and re-layouts: 1.42 us -> 0.62 us
    pallas_call x1, Pallas kernels: 48.9 us -> 48.3 us  [shards(): pl.pallas_call(functools.partial(kernel, nb, nw), out_shape=jax.ShapeDtyp...]
where the time goes in v5:
time: 49 us; the launch traced here: 48.9 us
  Pallas kernels  48.3 us (99%)
  local copies, waits for them, and re-layouts  0.62 us (1%)
    pallas_call x1, Pallas kernels, shards(): pl.pallas_call(functools.partial(kernel, nb, nw), out_shape=jax.ShapeDtyp...  48.3 us

profile of v5, /device:TPU:1, one launch (start us, length us, event | category | flops | bytes accessed | tf_op | source)
XLA Modules:
  0.0 48.9 jit_solution(13157621806600497153)
XLA Ops:
  0.0 48.3 %shard_map.64 = f32[48,256]{1,0:T(8,128)S(1)} custom-call(f32[48,256]{1,0:T(8,128)} %log_hbm.1, f32[48,256]{1,0:T(8,128)} %lw_hbm.1, s32[48,256]{1,0:T(8,128)} %bits_hbm.1, bf16[25,24,25]{2,1,0:T(8,128)(2,1)} %bitcast.2, f32[12]{0:T(128)} %gain_hbm.1, s32[1,2,1,16]{3,2,1,0:T(1,128)} %bitcast.3), custom_call_target="tpu_custom_call" | custom-call | tf_op jit(solution)/shard_map/pallas_call | solution.py:358
  48.3 0.6 %copy.8 = f32[48,256]{1,0:T(8,128)} copy(f32[48,256]{1,0:T(8,128)S(1)} %shard_map.64) | data formatting | bytes 98304

commit v6 on v5

--- a/solution.py
+++ b/solution.py
@@ -296,10 +296,6 @@
         own_soft = sigmoid(frame[0, OWN_R : OWN_R + H, OWN_C : OWN_C + W])
         gradient = (own[...] + last) * own_soft * (1.0 - own_soft)
         own[...] = gradient
-        if step < ITERS - 1:
-            copies_g = rims(gframe.at[pl.ds(step, 1), OWN_R : OWN_R + H, OWN_C : OWN_C + W], gframe.at[pl.ds(step, 1)], g_send, g_recv)
-            sends += copies_g
-
         squares = jnp.sum(gradient * gradient, axis=0, keepdims=True)
         squares = squares[:, :128] + squares[:, 128:]
 
@@ -328,6 +324,9 @@
                 pl.semaphore_wait(knows_all, len(far))
             squares, every = reduce(squares, 3 * step + at, slots, order, me, device)
             sends.append(every)
+            if at == 0 and step < ITERS - 1:
+                copies_g = rims(gframe.at[pl.ds(step, 1), OWN_R : OWN_R + H, OWN_C : OWN_C + W], gframe.at[pl.ds(step, 1)], g_send, g_recv)
+                sends += copies_g
         mean = jnp.sum(squares, axis=1, keepdims=True) * (1.0 / (nb * nw * H * W))
         scale = STEP_SIZE / jnp.sqrt(mean + EPSILON)
         if step < ITERS - 1:

time: 49 us -> 49.2 us (level)
  no operation moved by 1% of the time
where the time goes in v6:
time: 49.2 us; the launch traced here: 49.1 us
  Pallas kernels  48.5 us (99%)
  local copies, waits for them, and re-layouts  0.62 us (1%)
    pallas_call x1, Pallas kernels, shards(): pl.pallas_call(functools.partial(kernel, nb, nw), out_shape=jax.ShapeDtyp...  48.5 us

profile of v6, /device:TPU:1, one launch (start us, length us, event | category | flops | bytes accessed | tf_op | source)
XLA Modules:
  0.0 49.1 jit_solution(3018870058125169134)
XLA Ops:
  0.0 48.5 %shard_map.64 = f32[48,256]{1,0:T(8,128)S(1)} custom-call(f32[48,256]{1,0:T(8,128)} %log_hbm.1, f32[48,256]{1,0:T(8,128)} %lw_hbm.1, s32[48,256]{1,0:T(8,128)} %bits_hbm.1, bf16[25,24,25]{2,1,0:T(8,128)(2,1)} %bitcast.2, f32[12]{0:T(128)} %gain_hbm.1, s32[1,2,1,16]{3,2,1,0:T(1,128)} %bitcast.3), custom_call_target="tpu_custom_call" | custom-call | tf_op jit(solution)/shard_map/pallas_call | solution.py:357
  48.5 0.6 %copy.8 = f32[48,256]{1,0:T(8,128)} copy(f32[48,256]{1,0:T(8,128)S(1)} %shard_map.64) | data formatting | bytes 98304
